TPU v7x, 128 devices: a whole 4x4x4 slice. The times are simulated.
128 devices in a mesh: section: 16 (over z, y_lo, core), tensor: 8 (over y_hi, x).
Axes of the slice: x: 4, y: 4 (y_hi: 2, y_lo: 2; y = y_hi * 2 + y_lo), z: 4, core: 2. Of those that a mesh axis runs over, the one named last changes fastest.
Arguments:
- token_ids: int32 [4096], P('section'), may hold values from 0 to 152063, as said below
- column_order: int32 [8192], replicated, may hold values from 0 to 8191, each once
- residual: bfloat16 [4096, 8192], P('section', 'tensor'), may hold values from -40 to 40
- attn_out: bfloat16 [4096, 8192], P('section', 'tensor'), may hold values from -6 to 6
- out_proj: bfloat16 [8192, 8192], P(None, 'tensor'), may hold values from -0.0625 to 0.0625
- norm_gain: float32 [8192], P('tensor'), may hold values from 0.5 to 1.5
Outputs:
- factored: float32 [8192, 8192], P('section', 'tensor')
Inputs may be any that keep to these rules, and one draw needn't show every extreme that they name: `token_ids`: id 0 marks padding. In each block of 256 tokens of one section index the padding fills trailing positions, and each block holds at least one non-padding token.
All inputs are finite; a program needn't handle non-finite values.
Results may differ from a plain program's by a relative error of at most 0.0067.
Values may be sent and summed in bfloat16 or wider, within the bound.
No kernel may reach another device: no remote copies, remote signals or barrier semaphores. Data moves between devices by JAX's collectives and lax.ppermute only.
A program may use at most 128 MiB of HBM per device.

v0:
```python
import jax
import jax.numpy as jnp
from jax import lax
from jax.sharding import PartitionSpec as P

TILE = 128
PANEL = 1024
epsilon = 1e-06


def spread(value, axis, source):
    kept = jnp.where(lax.axis_index(axis) == source, value, 0).astype(value.dtype)
    return lax.psum(kept, axis)


def shards(token_ids, column_order, residual, attn_out, out_proj, norm_gain):
    section_count = lax.axis_size("section")
    tensor_count = lax.axis_size("tensor")
    section_id = lax.axis_index("section")
    tensor_id = lax.axis_index("tensor")
    model_width = out_proj.shape[0]
    span_rows = model_width // section_count
    span_cols = model_width // tensor_count
    projected = jnp.dot(
        lax.all_gather(attn_out, "tensor", axis=1, tiled=True),
        out_proj,
        preferred_element_type=jnp.float32,
    )
    rounded = (residual.astype(jnp.float32) + projected).astype(jnp.bfloat16)
    hidden = lax.optimization_barrier(rounded).astype(jnp.float32)
    squares = lax.psum(jnp.sum(hidden * hidden, axis=1), "tensor")
    kept_rows = (token_ids != 0).astype(jnp.float32)
    token_count = lax.psum(jnp.sum(kept_rows), "section")
    row_scale = lax.rsqrt(squares / model_width + epsilon) * kept_rows
    normed = (hidden * row_scale[:, None] * norm_gain[None, :]).astype(jnp.bfloat16)
    target = jnp.arange(section_count, dtype=jnp.int32)[:, None, None]
    tile_index = jnp.arange(span_rows // TILE, dtype=jnp.int32)[None, :, None]
    offset = jnp.arange(TILE, dtype=jnp.int32)[None, None, :]
    send_global = ((tile_index * section_count + target) * TILE + offset).reshape(model_width)
    col_tiles = jnp.arange(span_cols // TILE, dtype=jnp.int32)[:, None]
    cols_global = (
        (col_tiles * tensor_count + tensor_id) * TILE + jnp.arange(TILE, dtype=jnp.int32)[None, :]
    ).reshape(span_cols)
    full_rows = lax.all_gather(normed, "tensor", axis=1, tiled=True)
    outgoing = jnp.take(full_rows, jnp.take(column_order, send_global), axis=1)
    mine_rows = lax.all_to_all(outgoing, "section", split_axis=1, concat_axis=0, tiled=True)
    col_part = jnp.take(full_rows, jnp.take(column_order, cols_global), axis=1)
    gram_sum = lax.dot_general(
        mine_rows,
        lax.all_gather(col_part, "section", axis=0, tiled=True),
        (((0,), (0,)), ((), ())),
        preferred_element_type=jnp.float32,
    )
    hessian = gram_sum / token_count
    panel_local = PANEL // tensor_count
    per_group = panel_local // TILE
    gathered = lax.all_gather(hessian[:, :panel_local], "tensor", axis=1, tiled=True)
    panel_rows = (
        gathered.reshape(span_rows, tensor_count, per_group, TILE)
        .transpose(0, 2, 1, 3)
        .reshape(span_rows, PANEL)
    )
    first_tile = panel_rows[:TILE]
    stacked = lax.all_gather(first_tile, "section", axis=0, tiled=True)
    diag_block = stacked[:PANEL]
    chol_low = jnp.linalg.cholesky(diag_block)
    own_lower = lax.linalg.triangular_solve(
        chol_low, panel_rows, left_side=False, lower=True, transpose_a=True
    )
    copies = [
        spread(own_lower, "section", tensor_id + second * tensor_count)
        for second in range(section_count // tensor_count)
    ]
    shaped = [copy_rows.reshape(span_rows // TILE, TILE, PANEL) for copy_rows in copies]
    other_lower = jnp.stack(shaped, axis=1).reshape(span_cols, PANEL)
    row_tiles = jnp.arange(span_rows // TILE, dtype=jnp.int32)[:, None]
    rows_global = (
        (row_tiles * section_count + section_id) * TILE + jnp.arange(TILE, dtype=jnp.int32)[None, :]
    ).reshape(span_rows)
    panel_global = cols_global[:panel_local]
    left_part = jnp.take(own_lower, panel_global, axis=1)
    left_part = jnp.where(
        rows_global[:, None] >= panel_global[None, :], left_part, jnp.float32(0.0)
    )
    update = jnp.dot(
        own_lower,
        other_lower[panel_local:].T,
        precision=lax.Precision.HIGHEST,
        preferred_element_type=jnp.float32,
    )
    right_part = hessian[:, panel_local:] - update
    return jnp.concatenate([left_part, right_part], axis=1)


def solution(mesh):
    placed = (
        P("section"),
        P(),
        P("section", "tensor"),
        P("section", "tensor"),
        P(None, "tensor"),
        P("tensor"),
    )
    return jax.shard_map(
        shards, mesh=mesh, in_specs=placed, out_specs=P("section", "tensor"), check_vma=False
    )
```

profile of v0, /device:TPU:0, one launch (start us, length us, event | category | flops | bytes accessed | tf_op | source)
XLA Modules:
  0.0 999.8 jit_solution(9918803187925176559)
XLA Ops:
  7.3 76.3 %all-gather.6.cloned.1.call-done = bf16[256,8192]{1,0:T(8,128)(2,1)} async-done(((bf16[256,1024]{1,0:T(8,128)(2,1)}), bf16[256,8192]{1,0:T(8,128)(2,1)}) %all-gather.6.cloned.1.call-update) | async-done | bytes 4194320 | tf_op jit(solution)/shard_map/all_gather | solution.py:25
  83.7 11.5 %fusion.5 = bf16[256,1024]{1,0:T(8,128)(2,1)S(1)} fusion(bf16[256,8192]{1,0:T(8,128)(2,1)} %all-gather.6.cloned.1.call-done, bf16[8192,1024]{1,0:T(8,128)(2,1)} %param.10, bf16[256,1024]{1,0:T(8,128)(2,1)} %param.8), kind=kOutput, calls=%fused_computation.21 | convolution fusion | flops 4295753728 | bytes 22020096 | tf_op jit(solution)/shard_map/dot_general | solution.py:24
  95.3 19.8 %psum.28 = f32[256]{0:T(256)S(1)} all-reduce(f32[256]{0:T(256)S(1)} %fusion.6), channel_id=1, replica_groups=mesh['section'=16,'tensor'=8] {'tensor'}, use_global_device_ids=true, to_apply=%region_1.0 | all-reduce | flops 256 | bytes 2048 | tf_op jit(solution)/shard_map/psum | solution.py:31
  123.2 64.0 %all-gather.8.cloned.1.call-done = bf16[256,8192]{1,0:T(8,128)(2,1)} async-done(((bf16[256,1024]{1,0:T(8,128)(2,1)}), bf16[256,8192]{1,0:T(8,128)(2,1)}) %all-gather.8.cloned.1.call-update) | async-done | bytes 4194320 | tf_op jit(solution)/shard_map/all_gather | solution.py:44
  201.0 45.5 %gather_fusion = s32[8192]{0:T(1024)S(1)} fusion(s32[8192]{0:T(1024)S(1)} %copy-done, s32[8192]{0:T(1024)S(1)} %broadcast_clamp_fusion.1), kind=kCustom, calls=%fused_computation | custom fusion | bytes 98304 | tf_op jit(solution)/shard_map/jit(_take)/gather | solution.py:45
  246.7 33.9 %gather_fusion.1 = bf16[8192,256]{1,0:T(8,128)(2,1)} fusion(bf16[256,8192]{0,1:T(8,128)(2,1)} %copy.13, s32[8192]{0:T(1024)S(1)} %broadcast_clamp_fusion), kind=kCustom, calls=%fused_computation.1 | custom fusion | bytes 8421376 | tf_op jit(solution)/shard_map/jit(_take)/gather | solution.py:45
  296.2 72.6 %psum.29 = f32[]{:T(128)} all-reduce(f32[]{:T(128)} %get-tuple-element.74), channel_id=1, replica_groups=mesh['section'=16,'tensor'=8] {'section'}, use_global_device_ids=true, to_apply=%region_3.0 | all-reduce | flops 1 | bytes 8 | tf_op jit(solution)/shard_map/psum | solution.py:33
  379.8 51.4 %all-gather.12.cloned.1.call-done = f32[512,1024]{0,1:T(8,128)} async-done(((f32[512,128]{0,1:T(8,128)}), f32[512,1024]{0,1:T(8,128)}) %all-gather.12.cloned.1.call-update) | async-done | bytes 2097168 | tf_op jit(solution)/shard_map/all_gather | solution.py:57
  433.3 59.7 %all-gather.14.cloned.1.call-done = f32[2048,1024]{0,1:T(8,128)} async-done(((f32[128,1024]{0,1:T(8,128)}), f32[2048,1024]{0,1:T(8,128)}) %all-gather.14.cloned.1.call-update) | async-done | bytes 8388624 | tf_op jit(solution)/shard_map/all_gather | solution.py:64
  509.7 11.7 %cholesky.223 = f32[128,128]{1,0:T(8,128)S(1)} custom-call(f32[128,128]{1,0:T(8,128)S(1)} %cholesky.580), custom_call_target="Cholesky" | custom-call | tf_op jit(solution)/shard_map/jit(cholesky)/cholesky | solution.py:66
  521.5 9.8 custom-call.62
  537.8 11.9 %cholesky.244 = f32[128,128]{1,0:T(8,128)S(1)} custom-call(f32[128,128]{1,0:T(8,128)S(1)} %cholesky.584), custom_call_target="Cholesky" | custom-call | tf_op jit(solution)/shard_map/jit(cholesky)/cholesky | solution.py:66
  550.3 9.8 custom-call.63
  563.5 11.7 %cholesky.468 = f32[128,128]{1,0:T(8,128)S(1)} custom-call(f32[128,128]{1,0:T(8,128)S(1)} %cholesky.589), custom_call_target="Cholesky" | custom-call | tf_op jit(solution)/shard_map/jit(cholesky)/cholesky | solution.py:66
  576.5 9.8 custom-call.64
  589.8 12.1 %cholesky.487 = f32[128,128]{1,0:T(8,128)S(1)} custom-call(f32[128,128]{1,0:T(8,128)S(1)} %cholesky.594), custom_call_target="Cholesky" | custom-call | tf_op jit(solution)/shard_map/jit(cholesky)/cholesky | solution.py:66
  616.5 11.7 %cholesky.506 = f32[128,128]{1,0:T(8,128)S(1)} custom-call(f32[128,128]{1,0:T(8,128)S(1)} %cholesky.599), custom_call_target="Cholesky" | custom-call | tf_op jit(solution)/shard_map/jit(cholesky)/cholesky | solution.py:66
  629.5 9.9 custom-call.66
  642.7 11.7 %cholesky.526 = f32[128,128]{1,0:T(8,128)S(1)} custom-call(f32[128,128]{1,0:T(8,128)S(1)} %cholesky.604), custom_call_target="Cholesky" | custom-call | tf_op jit(solution)/shard_map/jit(cholesky)/cholesky | solution.py:66
  668.6 11.9 %cholesky.546 = f32[128,128]{1,0:T(8,128)S(1)} custom-call(f32[128,128]{1,0:T(8,128)S(1)} %cholesky.609), custom_call_target="Cholesky" | custom-call | tf_op jit(solution)/shard_map/jit(cholesky)/cholesky | solution.py:66
  694.3 11.7 %cholesky.564 = f32[128,128]{1,0:T(8,128)S(1)} custom-call(f32[128,128]{1,0:T(8,128)S(1)} %convolution_subtract_fusion.13), custom_call_target="Cholesky" | custom-call | tf_op jit(solution)/shard_map/jit(cholesky)/cholesky | solution.py:66
  717.8 22.9 %while.1 = (s32[]{:T(128)}, f32[1024,1024]{1,0:T(8,128)}, s32[8,2]{0,1:T(2,128)S(1)}, f32[8,128,128]{2,1,0:T(8,128)S(1)}, s32[]{:T(128)}) while((s32[]{:T(128)}, f32[1024,1024]{1,0:T(8,128)}, s32[8,2]{0,1:T(2,128)S(1)}, f32[8,128,128]{2,1,0:T(8,128)S(1)}, s32[]{:T(128)}) %tuple.59), condition=%wide.while_cond, body=%wide.while_body.sunk | while | flops 2 | bytes 131181 | solution.py:67
  740.7 79.0 %custom-call.69 = f32[8,128,128]{1,2,0:T(8,128)S(1)} custom-call(f32[8,128,128]{2,1,0:T(8,128)S(1)} %get-tuple-element.12), custom_call_target="InvertDiagBlocksLowerTriangular" | custom-call | tf_op jit(solution)/shard_map/triangular_solve | solution.py:67
  846.5 135.4 %all-reduce.4.cloned.1.call-done = (f32[4,1,128,1024]{3,2,1,0:T(8,128)}, f32[4,1,128,1024]{3,2,1,0:T(8,128)}) async-done(((f32[4,1,128,1024]{3,2,1,0:T(8,128)}, f32[4,1,128,1024]{3,2,1,0:T(8,128)}), (f32[4,1,128,1024]{3,2,1,0:T(8,128)}, f32[4,1,128,1024]{3,2,1,0:T(8,128)})) %all-reduce.4.cloned.1.call-update) | async-done | bytes 4194320 | tf_op jit(solution)/shard_map/psum | solution.py:13
  (160 shorter events, 197.5 us)
Async XLA Ops:
  6.5 110.4 %copy-start = (s32[8192]{0:T(1024)S(1)}, s32[8192]{0:T(1024)}, u32[]{:S(2)}) copy-start(s32[8192]{0:T(1024)} %param.7) | copy-start | bytes 98308
  6.5 77.1 %all-gather.6.cloned.1.call-start = ((), (), s32[]{:S(2)}) async-start(), calls=%async_computation.1 | async-start | bytes 4718592 | tf_op jit(solution)/shard_map/all_gather | solution.py:25
  7.3 107.8 %copy-start.7 = (s32[256]{0:T(256)S(1)}, s32[256]{0:T(256)}, u32[]{:S(2)}) copy-start(s32[256]{0:T(256)} %param.6) | copy-start | bytes 3076
  7.3 108.5 %copy-start.6 = (f32[1024]{0:T(1024)S(1)}, f32[1024]{0:T(1024)}, u32[]{:S(2)}) copy-start(f32[1024]{0:T(1024)} %param.11) | copy-start | bytes 12292
  7.3 180.0 %all-gather.8.cloned.1.call-start = ((), (), s32[]{:S(2)}) async-start(), calls=%async_computation.2 | async-start | bytes 4718592 | tf_op jit(solution)/shard_map/all_gather | solution.py:44
  116.8 252.1 %all-gather.10.cloned.1.call-start = ((), (), s32[]{:S(2)}) async-start(), calls=%async_computation.3 | async-start | bytes 8912896 | tf_op jit(solution)/shard_map/all_gather | solution.py:50
  291.6 77.3 %all-to-all-start = ((bf16[256,16,512]{2,0,1:T(8,128)(2,1)}), bf16[256,16,512]{2,0,1:T(8,128)(2,1)}, u32[]{:S(2)}, u32[]{:S(2)}) async-start(bf16[256,16,512]{2,0,1:T(8,128)(2,1)} %broadcast_select_fusion), calls=%async_computation | async-start | bytes 8388608 | tf_op jit(solution)/shard_map/all_to_all | solution.py:46
  296.2 135.1 %all-gather.12.cloned.1.call-start = ((), (), s32[]{:S(2)}) async-start(), calls=%async_computation.4 | async-start | bytes 2359296 | tf_op jit(solution)/shard_map/all_gather | solution.py:57
  377.7 1.3 copy-start.3
  379.8 113.2 %all-gather.14.cloned.1.call-start = ((), (), s32[]{:S(2)}) async-start(), calls=%async_computation.5 | async-start | bytes 8912896 | tf_op jit(solution)/shard_map/all_gather | solution.py:64
  433.2 548.8 %all-reduce.4.cloned.1.call-start = ((), (), s32[]{:S(2)}) async-start(), calls=%async_computation.6 | async-start | bytes 8388608 | tf_op jit(solution)/shard_map/psum | solution.py:13
  507.7 2.0 copy-start.2
  821.1 6.1 copy-start.5
  981.9 2.9 copy-start.4
  984.8 8.0 copy-start.1
Sparse Core Ops, SparseCore 0:
  9.7 73.9 all-gather.5
  116.9 70.3 all-gather.7
  201.0 58.7 all-gather.9
  379.9 51.3 all-gather.11
  433.3 59.6 all-gather.13
  845.7 136.2 all-reduce.3
where the time goes:
time: 1010 us; the launch traced here: 1000 us
  waiting for transfers between devices  388 us (38%)
  other arithmetic  274 us (27%)
  local copies, waits for them, and re-layouts  155 us (15%)
  blocking collectives  92.4 us (9%)
  matrix products  66.5 us (7%)
  between operations  19.2 us (2%)
    another operation x30, other arithmetic, shards(): chol_low = jnp.linalg.cholesky(diag_block)  172 us
    psum x1, waiting for transfers between devices, spread(): return lax.psum(kept, axis)  135 us
    gather x4, local copies, waits for them, and re-layouts, shards(): outgoing = jnp.take(full_rows, jnp.take(column_order, send_global), axis=1)  85.8 us
    another operation x3, other arithmetic, shards(): lax.linalg.triangular_solve(chol_low, panel_rows, left_side=False, lower=...  83.9 us
    all_gather x1, waiting for transfers between devices, shards(): lax.all_gather(attn_out, 'tensor', axis=1, tiled=True)  76.3 us
    psum x1, blocking collectives, shards(): token_count = lax.psum(jnp.sum(kept_rows), 'section')  72.6 us
    all_gather x1, waiting for transfers between devices, shards(): full_rows = lax.all_gather(normed, 'tensor', axis=1, tiled=True)  64 us
    all_gather x1, waiting for transfers between devices, shards(): stacked = lax.all_gather(first_tile, 'section', axis=0, tiled=True)  59.7 us
  transfers between devices with their start and end apart: 7, of which 5 were waited for; matrix products, arithmetic and copies ran while one was open for 10% of the time, Pallas kernels for 0%

commit v1 on v0

--- a/solution.py
+++ b/solution.py
@@ -61,7 +61,8 @@
         .reshape(span_rows, PANEL)
     )
     first_tile = panel_rows[:TILE]
-    stacked = lax.all_gather(first_tile, "section", axis=0, tiled=True)
+    stack = jnp.stack([first_tile] * lax.axis_size("section"))
+    stacked = jnp.concatenate(lax.all_to_all(stack, "section", 0, 0), axis=0)
     diag_block = stacked[:PANEL]
     chol_low = jnp.linalg.cholesky(diag_block)
     own_lower = lax.linalg.triangular_solve(

time: 1010 us -> 1070 us (1.059)
  waiting for transfers between devices: 388 us -> 424 us
  matrix products: 66.5 us -> 81.4 us
    all_to_all x0 -> x1, waiting for transfers between devices: none -> 95.2 us  [shards(): stacked = jnp.concatenate(lax.all_to_all(stack, 'section', 0, 0), axis=0)]
    all_gather x1 -> x0, waiting for transfers between devices: 59.7 us -> none  [shards(): stacked = lax.all_gather(first_tile, 'section', axis=0, tiled=True)]
    another operation x24 -> x25, local copies, waits for them, and re-layouts: 22.7 us -> 26.9 us
  transfers between devices with their start and end apart: 7 -> 7, of which waited for: 5 -> 5; matrix products, arithmetic and copies ran while one was open for 10% -> 9% of each run, Pallas kernels for 0% -> 0%
where the time goes in v1:
time: 1070 us; the launch traced here: 1060 us
  waiting for transfers between devices  424 us (40%)
  other arithmetic  275 us (26%)
  local copies, waits for them, and re-layouts  157 us (15%)
  blocking collectives  92.4 us (9%)
  matrix products  81.4 us (8%)
  between operations  19.1 us (2%)
    another operation x30, other arithmetic, shards(): chol_low = jnp.linalg.cholesky(diag_block)  172 us
    psum x1, waiting for transfers between devices, spread(): return lax.psum(kept, axis)  134 us
    all_to_all x1, waiting for transfers between devices, shards(): stacked = jnp.concatenate(lax.all_to_all(stack, 'section', 0, 0), axis=0)  95.2 us
    gather x4, local copies, waits for them, and re-layouts, shards(): outgoing = jnp.take(full_rows, jnp.take(column_order, send_global), axis=1)  85.8 us
    another operation x3, other arithmetic, shards(): lax.linalg.triangular_solve(chol_low, panel_rows, left_side=False, lower=...  83.7 us
    all_gather x1, waiting for transfers between devices, shards(): lax.all_gather(attn_out, 'tensor', axis=1, tiled=True)  76.3 us
    psum x1, blocking collectives, shards(): token_count = lax.psum(jnp.sum(kept_rows), 'section')  72.6 us
    all_gather x1, waiting for transfers between devices, shards(): full_rows = lax.all_gather(normed, 'tensor', axis=1, tiled=True)  64 us
  transfers between devices with their start and end apart: 7, of which 5 were waited for; matrix products, arithmetic and copies ran while one was open for 9% of the time, Pallas kernels for 0%

profile of v1, /device:TPU:0, one launch (start us, length us, event | category | flops | bytes accessed | tf_op | source)
XLA Modules:
  0.0 1058.3 jit_solution(16531233969611916458)
XLA Ops:
  7.3 76.3 %all-gather.5.cloned.1.call-done = bf16[256,8192]{1,0:T(8,128)(2,1)} async-done(((bf16[256,1024]{1,0:T(8,128)(2,1)}), bf16[256,8192]{1,0:T(8,128)(2,1)}) %all-gather.5.cloned.1.call-update) | async-done | bytes 4194320 | tf_op jit(solution)/shard_map/all_gather | solution.py:25
  83.7 11.5 %fusion.5 = bf16[256,1024]{1,0:T(8,128)(2,1)S(1)} fusion(bf16[256,8192]{1,0:T(8,128)(2,1)} %all-gather.5.cloned.1.call-done, bf16[8192,1024]{1,0:T(8,128)(2,1)} %param.10, bf16[256,1024]{1,0:T(8,128)(2,1)} %param.8), kind=kOutput, calls=%fused_computation.23 | convolution fusion | flops 4295753728 | bytes 22020096 | tf_op jit(solution)/shard_map/dot_general | solution.py:24
  95.3 19.8 %psum.28 = f32[256]{0:T(256)S(1)} all-reduce(f32[256]{0:T(256)S(1)} %fusion.6), channel_id=1, replica_groups=mesh['section'=16,'tensor'=8] {'tensor'}, use_global_device_ids=true, to_apply=%region_1.0 | all-reduce | flops 256 | bytes 2048 | tf_op jit(solution)/shard_map/psum | solution.py:31
  123.2 64.0 %all-gather.7.cloned.1.call-done = bf16[256,8192]{1,0:T(8,128)(2,1)} async-done(((bf16[256,1024]{1,0:T(8,128)(2,1)}), bf16[256,8192]{1,0:T(8,128)(2,1)}) %all-gather.7.cloned.1.call-update) | async-done | bytes 4194320 | tf_op jit(solution)/shard_map/all_gather | solution.py:44
  201.0 45.5 %gather_fusion = s32[8192]{0:T(1024)S(1)} fusion(s32[8192]{0:T(1024)S(1)} %copy-done, s32[8192]{0:T(1024)S(1)} %broadcast_clamp_fusion.1), kind=kCustom, calls=%fused_computation | custom fusion | bytes 98304 | tf_op jit(solution)/shard_map/jit(_take)/gather | solution.py:45
  246.7 33.9 %gather_fusion.1 = bf16[8192,256]{1,0:T(8,128)(2,1)} fusion(bf16[256,8192]{0,1:T(8,128)(2,1)} %copy.20, s32[8192]{0:T(1024)S(1)} %broadcast_clamp_fusion), kind=kCustom, calls=%fused_computation.1 | custom fusion | bytes 8421376 | tf_op jit(solution)/shard_map/jit(_take)/gather | solution.py:45
  296.2 72.6 %psum.29 = f32[]{:T(128)} all-reduce(f32[]{:T(128)} %get-tuple-element.74), channel_id=1, replica_groups=mesh['section'=16,'tensor'=8] {'section'}, use_global_device_ids=true, to_apply=%region_3.0 | all-reduce | flops 1 | bytes 8 | tf_op jit(solution)/shard_map/psum | solution.py:33
  379.9 54.0 %all-gather.11.cloned.1.call-done = f32[512,1024]{1,0:T(8,128)} async-done(((f32[512,128]{1,0:T(8,128)}), f32[512,1024]{1,0:T(8,128)}) %all-gather.11.cloned.1.call-update) | async-done | bytes 2097168 | tf_op jit(solution)/shard_map/all_gather | solution.py:57
  444.2 95.2 %all-to-all-done.1 = f32[16,128,1024]{1,2,0:T(8,128)} async-done(((f32[16,128,1024]{1,2,0:T(8,128)}), f32[16,128,1024]{1,2,0:T(8,128)}, u32[]{:S(2)}, u32[]{:S(2)}) %all-to-all-start.1) | async-done | bytes 8388640 | tf_op jit(solution)/shard_map/all_to_all | solution.py:65
  555.8 11.7 %cholesky.223 = f32[128,128]{1,0:T(8,128)S(1)} custom-call(f32[128,128]{1,0:T(8,128)S(1)} %cholesky.580), custom_call_target="Cholesky" | custom-call | tf_op jit(solution)/shard_map/jit(cholesky)/cholesky | solution.py:67
  567.5 9.8 custom-call.62
  583.8 11.7 %cholesky.244 = f32[128,128]{1,0:T(8,128)S(1)} custom-call(f32[128,128]{1,0:T(8,128)S(1)} %cholesky.584), custom_call_target="Cholesky" | custom-call | tf_op jit(solution)/shard_map/jit(cholesky)/cholesky | solution.py:67
  596.2 10.0 custom-call.63
  609.6 11.7 %cholesky.468 = f32[128,128]{1,0:T(8,128)S(1)} custom-call(f32[128,128]{1,0:T(8,128)S(1)} %cholesky.589), custom_call_target="Cholesky" | custom-call | tf_op jit(solution)/shard_map/jit(cholesky)/cholesky | solution.py:67
  635.9 12.1 %cholesky.487 = f32[128,128]{1,0:T(8,128)S(1)} custom-call(f32[128,128]{1,0:T(8,128)S(1)} %cholesky.594), custom_call_target="Cholesky" | custom-call | tf_op jit(solution)/shard_map/jit(cholesky)/cholesky | solution.py:67
  662.6 11.7 %cholesky.506 = f32[128,128]{1,0:T(8,128)S(1)} custom-call(f32[128,128]{1,0:T(8,128)S(1)} %cholesky.599), custom_call_target="Cholesky" | custom-call | tf_op jit(solution)/shard_map/jit(cholesky)/cholesky | solution.py:67
  688.9 11.7 %cholesky.526 = f32[128,128]{1,0:T(8,128)S(1)} custom-call(f32[128,128]{1,0:T(8,128)S(1)} %cholesky.604), custom_call_target="Cholesky" | custom-call | tf_op jit(solution)/shard_map/jit(cholesky)/cholesky | solution.py:67
  714.7 11.7 %cholesky.546 = f32[128,128]{1,0:T(8,128)S(1)} custom-call(f32[128,128]{1,0:T(8,128)S(1)} %cholesky.609), custom_call_target="Cholesky" | custom-call | tf_op jit(solution)/shard_map/jit(cholesky)/cholesky | solution.py:67
  727.7 10.1 custom-call.68
  740.5 11.7 %cholesky.564 = f32[128,128]{1,0:T(8,128)S(1)} custom-call(f32[128,128]{1,0:T(8,128)S(1)} %convolution_subtract_fusion.13), custom_call_target="Cholesky" | custom-call | tf_op jit(solution)/shard_map/jit(cholesky)/cholesky | solution.py:67
  764.1 22.9 %while.1 = (s32[]{:T(128)}, f32[1024,1024]{1,0:T(8,128)}, s32[8,2]{0,1:T(2,128)S(1)}, f32[8,128,128]{2,1,0:T(8,128)S(1)}, s32[]{:T(128)}) while((s32[]{:T(128)}, f32[1024,1024]{1,0:T(8,128)}, s32[8,2]{0,1:T(2,128)S(1)}, f32[8,128,128]{2,1,0:T(8,128)S(1)}, s32[]{:T(128)}) %tuple.59), condition=%wide.while_cond, body=%wide.while_body.sunk | while | flops 2 | bytes 131181 | solution.py:68
  787.0 78.8 %custom-call.69 = f32[8,128,128]{1,2,0:T(8,128)S(1)} custom-call(f32[8,128,128]{2,1,0:T(8,128)S(1)} %get-tuple-element.12), custom_call_target="InvertDiagBlocksLowerTriangular" | custom-call | tf_op jit(solution)/shard_map/triangular_solve | solution.py:68
  900.2 133.6 %all-reduce.4.cloned.1.call-done = (f32[4,1,128,1024]{3,2,1,0:T(8,128)}, f32[4,1,128,1024]{3,2,1,0:T(8,128)}) async-done(((f32[4,1,128,1024]{3,2,1,0:T(8,128)}, f32[4,1,128,1024]{3,2,1,0:T(8,128)}), (f32[4,1,128,1024]{3,2,1,0:T(8,128)}, f32[4,1,128,1024]{3,2,1,0:T(8,128)})) %all-reduce.4.cloned.1.call-update) | async-done | bytes 4194320 | tf_op jit(solution)/shard_map/psum | solution.py:13
  1036.7 13.1 %slice_subtract_fusion = f32[512,896]{1,0:T(8,128)S(1)} fusion(f32[512,1024]{1,0:T(8,128)S(1)} %copy-done.5, f32[512,1024]{0,1:T(8,128)S(1)} %convolution_dynamic-update-slice_fusion.2, f32[1024,1024]{1,0:T(8,128)S(1)} %bitcast.155), kind=kOutput, calls=%fused_computation.18 | convolution fusion | flops 5637603328 | bytes 9437184 | tf_op jit(solution)/shard_map/dot_general | solution.py:86
  (161 shorter events, 216.7 us)
Async XLA Ops:
  6.5 110.4 %copy-start = (s32[8192]{0:T(1024)S(1)}, s32[8192]{0:T(1024)}, u32[]{:S(2)}) copy-start(s32[8192]{0:T(1024)} %param.7) | copy-start | bytes 98308
  6.5 77.1 %all-gather.5.cloned.1.call-start = ((), (), s32[]{:S(2)}) async-start(), calls=%async_computation.2 | async-start | bytes 4718592 | tf_op jit(solution)/shard_map/all_gather | solution.py:25
  7.3 107.8 %copy-start.7 = (s32[256]{0:T(256)S(1)}, s32[256]{0:T(256)}, u32[]{:S(2)}) copy-start(s32[256]{0:T(256)} %param.6) | copy-start | bytes 3076
  7.3 108.5 %copy-start.6 = (f32[1024]{0:T(1024)S(1)}, f32[1024]{0:T(1024)}, u32[]{:S(2)}) copy-start(f32[1024]{0:T(1024)} %param.11) | copy-start | bytes 12292
  7.3 180.0 %all-gather.7.cloned.1.call-start = ((), (), s32[]{:S(2)}) async-start(), calls=%async_computation.3 | async-start | bytes 4718592 | tf_op jit(solution)/shard_map/all_gather | solution.py:44
  116.8 252.1 %all-gather.9.cloned.1.call-start = ((), (), s32[]{:S(2)}) async-start(), calls=%async_computation.4 | async-start | bytes 8912896 | tf_op jit(solution)/shard_map/all_gather | solution.py:50
  291.6 77.3 %all-to-all-start = ((bf16[256,16,512]{2,0,1:T(8,128)(2,1)}), bf16[256,16,512]{2,0,1:T(8,128)(2,1)}, u32[]{:S(2)}, u32[]{:S(2)}) async-start(bf16[256,16,512]{2,0,1:T(8,128)(2,1)} %broadcast_select_fusion), calls=%async_computation | async-start | bytes 8388608 | tf_op jit(solution)/shard_map/all_to_all | solution.py:46
  296.2 137.8 %all-gather.11.cloned.1.call-start = ((), (), s32[]{:S(2)}) async-start(), calls=%async_computation.5 | async-start | bytes 2359296 | tf_op jit(solution)/shard_map/all_gather | solution.py:57
  377.8 1.3 copy-start.4
  439.4 100.1 %all-to-all-start.1 = ((f32[16,128,1024]{1,2,0:T(8,128)}), f32[16,128,1024]{1,2,0:T(8,128)}, u32[]{:S(2)}, u32[]{:S(2)}) async-start(f32[16,128,1024]{1,2,0:T(8,128)} %stack.4), calls=%async_computation.1 | async-start | bytes 16777216 | tf_op jit(solution)/shard_map/all_to_all | solution.py:65
  444.1 589.7 %all-reduce.4.cloned.1.call-start = ((), (), s32[]{:S(2)}) async-start(), calls=%async_computation.6 | async-start | bytes 8388608 | tf_op jit(solution)/shard_map/psum | solution.py:13
  553.7 2.0 copy-start.2
  867.2 7.7 copy-start.3
  1033.8 2.9 copy-start.5
  1036.7 14.7 %copy-start.1 = (s32[8192]{0:T(1024)S(1)}, s32[8192]{0:T(1024)}, u32[]{:S(2)}) copy-start(s32[8192]{0:T(1024)} %param.7) | copy-start | bytes 98308
Sparse Core Ops, SparseCore 0:
  9.7 73.9 all-gather.4
  116.9 70.3 all-gather.6
  201.0 58.7 all-gather.8
  380.0 53.8 all-gather.10
  899.2 134.5 all-reduce.3
